TPU v7x, 32 devices: a whole 2x2x4 slice. The times are simulated.
32 devices in a mesh: dp: 8 (over y, x, core), expert: 4 (over z).
Axes of the slice: x: 2, y: 2, z: 4, core: 2. Of those that a mesh axis runs over, the one named last changes fastest.
Arguments:
- tokens: bfloat16 [8192, 2048], P(('dp', 'expert')), may hold values from -6 to 6
- expert_ids: int32 [8192, 2], P(('dp', 'expert')), may hold values from 0 to 7, all different within a row; in each aligned block of 256 rows (0 to 255, 256 to 511, ...) at most 80 rows name the same one
- gate_weights: float32 [8192, 2], P(('dp', 'expert')), may hold values from 0.1 to 1
- old_place: int32 [8], replicated, may hold values from 0 to 7, each once
- new_place: int32 [8], replicated, may hold values from 0 to 7, each once
- params: bfloat16 [8, 3, 2048, 1024], P('dp', None, None, 'expert'), may hold values from -5 to 5
- grads: bfloat16 [8, 3, 2048, 1024], P('dp', None, None, 'expert'), may hold values from -6 to 6
- first_moment: float32 [8, 3, 2048, 1024], P('dp', None, None, 'expert'), may hold values from -2 to 2
- second_moment: float32 [8, 3, 2048, 1024], P('dp', None, None, 'expert'), may hold values from 0.05 to 1
Outputs:
- mixed: bfloat16 [8192, 2048], P(('dp', 'expert'))
- new_params: bfloat16 [8, 3, 2048, 1024], P('dp', None, None, 'expert')
- new_first: float32 [8, 3, 2048, 1024], P('dp', None, None, 'expert')
- new_second: float32 [8, 3, 2048, 1024], P('dp', None, None, 'expert')
Inputs may be any that keep to these rules, and one draw needn't show every extreme that they name: `expert_ids`: each token names 2 different experts. Among the rows of one device no expert is named more than 80 times, and in every draw some device names some expert exactly 80 times. `old_place`: A permutation of the 8 experts. `new_place`: A permutation of the 8 experts.
All inputs are finite; a program needn't handle non-finite values.
Results may differ from a plain program's by a relative error of at most 0.0076.
Values may be sent and summed in bfloat16 or wider, within the bound.
A program may use at most 192 MiB of HBM per device.

v0:
```python
import math

import jax
import jax.numpy as jnp
from jax import lax
from jax.sharding import PartitionSpec as P

FF = 1024


adam_rate = 0.3
first_decay = 0.9
second_decay = 0.95
adam_count = 10.0
adam_eps = 1e-08


def adam_update(params, grads, first_moment, second_moment):
    grad_value = grads.astype(jnp.float32)
    new_first = first_decay * first_moment + (1.0 - first_decay) * grad_value
    new_second = second_decay * second_moment + (1.0 - second_decay) * grad_value * grad_value
    first_hat = new_first / (1.0 - first_decay**adam_count)
    second_hat = new_second / (1.0 - second_decay**adam_count)
    stepped = params.astype(jnp.float32) - adam_rate * first_hat / (jnp.sqrt(second_hat) + adam_eps)
    return (stepped.astype(jnp.bfloat16), new_first, new_second)


def inverse_of(placement):
    entries = placement.shape[0]
    return jnp.zeros((entries,), jnp.int32).at[placement].set(jnp.arange(entries, dtype=jnp.int32))


def relocate(leading, first_moment, second_moment, source):
    pieces = lax.axis_size("dp")
    spread = (
        lax.all_to_all(
            leading.reshape(pieces, -1).astype(jnp.float32),
            "dp",
            split_axis=0,
            concat_axis=0,
            tiled=True,
        ).astype(jnp.bfloat16),
        lax.all_to_all(
            first_moment.reshape(pieces, -1), "dp", split_axis=0, concat_axis=0, tiled=True
        ),
        lax.all_to_all(
            second_moment.reshape(pieces, -1), "dp", split_axis=0, concat_axis=0, tiled=True
        ),
    )
    return (
        lax.all_to_all(
            spread[0][source].astype(jnp.float32), "dp", split_axis=0, concat_axis=0, tiled=True
        ).astype(jnp.bfloat16),
        lax.all_to_all(spread[1][source], "dp", split_axis=0, concat_axis=0, tiled=True),
        lax.all_to_all(spread[2][source], "dp", split_axis=0, concat_axis=0, tiled=True),
    )


def local(
    tokens,
    expert_ids,
    gate_weights,
    old_place,
    new_place,
    params,
    grads,
    first_moment,
    second_moment,
):
    experts = old_place.shape[0]
    tok_rows, features = tokens.shape
    topk = expert_ids.shape[1]
    capacity = 5 * tok_rows * topk // (4 * experts)
    source = inverse_of(old_place)[new_place]
    leading = jnp.stack([params, grads])
    delivered = relocate(leading, first_moment, second_moment, source)
    weight_pair = delivered[0].reshape((2,) + params.shape)
    new_params, new_first, new_second = adam_update(
        weight_pair[0],
        weight_pair[1],
        delivered[1].reshape(first_moment.shape),
        delivered[2].reshape(second_moment.shape),
    )
    flat_ids = expert_ids.reshape(-1)
    onehot = (flat_ids[:, None] == jnp.arange(experts, dtype=jnp.int32)[None, :]).astype(jnp.int32)
    slot_rank = jnp.sum((jnp.cumsum(onehot, axis=0) - 1) * onehot, axis=1)
    route_row = inverse_of(new_place)[flat_ids]
    slot_index = route_row * capacity + slot_rank
    slot_token = (
        jnp.full((experts * capacity,), -1, jnp.int32)
        .at[slot_index]
        .set(jnp.arange(flat_ids.shape[0], dtype=jnp.int32) // topk)
    )
    filled = slot_token >= 0
    outgoing = jnp.where(
        filled[:, None], tokens[jnp.maximum(slot_token, 0)], jnp.zeros((), jnp.bfloat16)
    )
    arrived = lax.all_to_all(
        outgoing.reshape(experts, capacity, features), "dp", split_axis=0, concat_axis=0, tiled=True
    ).reshape(-1, features)
    in_scale = 1.0 / math.sqrt(features)
    out_scale = 1.0 / math.sqrt(FF)
    columns = lax.all_gather(new_params[0], "expert", axis=2, tiled=True)
    gate_part = jnp.dot(arrived, columns[0], preferred_element_type=jnp.float32) * in_scale
    up_part = jnp.dot(arrived, columns[1], preferred_element_type=jnp.float32) * in_scale
    hidden = (jax.nn.silu(gate_part) * up_part).astype(jnp.bfloat16)
    summed = lax.dot_general(
        hidden, columns[2], (((1,), (1,)), ((), ())), preferred_element_type=jnp.float32
    )
    expert_out = (summed * out_scale).astype(jnp.bfloat16)
    returned = lax.all_to_all(
        expert_out.reshape(experts, capacity, features),
        "dp",
        split_axis=0,
        concat_axis=0,
        tiled=True,
    ).reshape(-1, features)
    picked = returned[slot_index].astype(jnp.float32).reshape(tok_rows, topk, features)
    mixed_out = jnp.sum(picked * gate_weights[:, :, None], axis=1).astype(jnp.bfloat16)
    return (mixed_out, new_params, new_first, new_second)


def solution(mesh):
    return jax.shard_map(
        local,
        mesh=mesh,
        in_specs=(
            P(("dp", "expert"), None),
            P(("dp", "expert"), None),
            P(("dp", "expert"), None),
            P(),
            P(),
            P("dp", None, None, "expert"),
            P("dp", None, None, "expert"),
            P("dp", None, None, "expert"),
            P("dp", None, None, "expert"),
        ),
        out_specs=(
            P(("dp", "expert"), None),
            P("dp", None, None, "expert"),
            P("dp", None, None, "expert"),
            P("dp", None, None, "expert"),
        ),
        check_vma=False,
    )
```

profile of v0, /device:TPU:0, one launch (start us, length us, event | category | flops | bytes accessed | tf_op | source)
XLA Modules:
  0.0 926.4 jit_solution(2082675422537184148)
XLA Ops:
  7.2 6.2 maximum_convert_fusion
  13.4 9.4 %reshape.319 = bf16[8,1,393216]{2,1,0:T(2,128)(2,1)} reshape(bf16[2,1,3,2048,256]{4,3,2,1,0:T(8,128)(2,1)} %maximum_convert_fusion) | data formatting | bytes 12582912 | tf_op jit(solution)/shard_map/convert_element_type | solution.py:37
  23.3 40.2 %reduce.16 = bf16[8,393216]{1,0:T(8,128)(2,1)} reduce(bf16[8,1,393216]{2,1,0:T(2,128)(2,1)} %reshape.319, bf16[]{:T(256)} %broadcast.346), dimensions={1}, to_apply=%reshape.319.reduce_sub_computation | reduce | bytes 12582914 | tf_op jit(solution)/shard_map/convert_element_type | solution.py:37
  63.5 11.5 %reshape.502 = bf16[8,2,196608]{2,1,0:T(2,128)(2,1)} reshape(bf16[8,393216]{1,0:T(8,128)(2,1)} %reduce.16) | data formatting | bytes 12582912
  80.1 10.5 %all_to_all.50 = f32[8,1,196608]{2,1,0:T(1,128)} reshape(f32[1,3,2048,256]{3,2,1,0:T(8,128)} %param.17) | data formatting | bytes 12582912 | tf_op jit(solution)/shard_map/all_to_all | solution.py:46
  90.6 10.5 %all_to_all.45 = f32[8,1,196608]{2,1,0:T(1,128)} reshape(f32[1,3,2048,256]{3,2,1,0:T(8,128)} %param.16) | data formatting | bytes 12582912 | tf_op jit(solution)/shard_map/all_to_all | solution.py:43
  101.2 10.5 %scatter_custom_fusion.2 = s32[8]{0:T(128)S(1)} fusion(s32[8]{0:T(128)S(1)} %compare_select_fusion.9, s32[8]{0:T(128)S(1)} %iota.19, s32[]{:T(128)} %constant.20.clone.1), kind=kCustom, calls=%fused_computation.89 | custom fusion | bytes 36 | tf_op jit(solution)/shard_map/scatter | solution.py:30
  112.9 39.1 %all-to-all-done.1 = bf16[8,2,196608]{2,1,0:T(2,128)(2,1)} async-done(((bf16[8,2,196608]{2,1,0:T(2,128)(2,1)}), bf16[8,2,196608]{2,1,0:T(2,128)(2,1)}, u32[]{:S(2)}, u32[]{:S(2)}) %all-to-all-start.1) | async-done | bytes 6291488 | tf_op jit(solution)/shard_map/all_to_all | solution.py:36
  156.8 11.0 %reshape.503 = bf16[8,1,393216]{2,1,0:T(2,128)(2,1)} reshape(bf16[8,2,196608]{2,1,0:T(2,128)(2,1)} %all-to-all-done.1) | data formatting | bytes 12582912
  167.8 12.0 %copy.33 = bf16[8,1,393216]{2,0,1:T(8,128)(2,1)S(1)} copy(bf16[8,1,393216]{2,1,0:T(2,128)(2,1)} %reshape.503) | data formatting | bytes 12582912 | tf_op jit(solution)/shard_map/all_to_all | solution.py:36
  182.0 5.6 gather_fusion.6
  187.6 5.6 gather_fusion.5
  193.3 5.6 gather_fusion.4
  201.6 11.7 %fusion.10 = bf16[8,1,393216]{2,0,1:T(8,128)(2,1)} fusion(bf16[8,98304]{1,0:T(8,128)(2,1)} %gather_fusion.6, bf16[8,98304]{1,0:T(8,128)(2,1)} %gather_fusion.5, bf16[8,98304]{1,0:T(8,128)(2,1)} %gather_fusion.4, bf16[8,98304]{1,0:T(8,128)(2,1)} %gather_fusion.3), kind=kLoop, calls=%fused_computation.31 | loop fusion | flops 25165824 | bytes 12582912 | tf_op jit(solution)/shard_map/convert_element_type | solution.py:52
  213.3 15.1 %all-to-all-done.5 = f32[8,1,196608]{2,1,0:T(1,128)} async-done(((f32[8,1,196608]{2,1,0:T(1,128)}), f32[8,1,196608]{2,1,0:T(1,128)}, u32[]{:S(2)}, u32[]{:S(2)}) %all-to-all-start.5) | async-done | bytes 6291488 | tf_op jit(solution)/shard_map/all_to_all | solution.py:46
  233.2 6.8 copy.34
  243.1 9.4 %reduce.17 = bf16[8,393216]{1,0:T(8,128)(2,1)} reduce(bf16[8,1,393216]{2,0,1:T(8,128)(2,1)} %fusion.10, bf16[]{:T(256)} %broadcast.346), dimensions={1}, to_apply=%copy.22.reduce_sub_computation | reduce | bytes 12582914 | tf_op jit(solution)/shard_map/convert_element_type | solution.py:52
  252.5 11.5 %reshape.504 = bf16[8,2,196608]{2,1,0:T(2,128)(2,1)} reshape(bf16[8,393216]{1,0:T(8,128)(2,1)} %reduce.17) | data formatting | bytes 12582912
  263.9 6.3 gather_fusion.10
  270.2 6.3 gather_fusion.9
  276.5 28.3 %all-to-all-done.3 = f32[8,1,196608]{2,1,0:T(1,128)} async-done(((f32[8,1,196608]{2,1,0:T(1,128)}), f32[8,1,196608]{2,1,0:T(1,128)}, u32[]{:S(2)}, u32[]{:S(2)}) %all-to-all-start.3) | async-done | bytes 6291488 | tf_op jit(solution)/shard_map/all_to_all | solution.py:43
  309.8 6.8 copy.35
  325.4 14.0 %copy.24 = f32[8,1,196608]{2,1,0:T(1,128)} copy(f32[8,1,196608]{2,0,1:T(8,128)S(1)} %maximum_bitcast_fusion.2) | data formatting | bytes 12582912 | tf_op jit(solution)/shard_map/all_to_all | solution.py:55
  339.4 6.3 gather_fusion.8
  345.7 6.3 gather_fusion.7
  352.0 29.4 %all-to-all-done.2 = bf16[8,2,196608]{2,1,0:T(2,128)(2,1)} async-done(((bf16[8,2,196608]{2,1,0:T(2,128)(2,1)}), bf16[8,2,196608]{2,1,0:T(2,128)(2,1)}, u32[]{:S(2)}, u32[]{:S(2)}) %all-to-all-start.2) | async-done | bytes 6291488 | tf_op jit(solution)/shard_map/all_to_all | solution.py:51
  390.0 14.1 %copy.23 = f32[8,1,196608]{2,1,0:T(1,128)} copy(f32[8,1,196608]{2,0,1:T(8,128)S(1)} %maximum_bitcast_fusion.1) | data formatting | bytes 12582912 | tf_op jit(solution)/shard_map/all_to_all | solution.py:54
  404.0 53.9 %all-to-all-done.6 = f32[8,1,196608]{2,1,0:T(1,128)} async-done(((f32[8,1,196608]{2,1,0:T(1,128)}), f32[8,1,196608]{2,1,0:T(1,128)}, u32[]{:S(2)}, u32[]{:S(2)}) %all-to-all-start.6) | async-done | bytes 6291488 | tf_op jit(solution)/shard_map/all_to_all | solution.py:55
  462.8 11.0 %reshape.505 = bf16[8,1,393216]{2,1,0:T(2,128)(2,1)} reshape(bf16[8,2,196608]{2,1,0:T(2,128)(2,1)} %all-to-all-done.2) | data formatting | bytes 12582912
  473.8 44.4 %fusion.8 = (f32[4,393216]{1,0:T(4,128)}, f32[4,393216]{1,0:T(4,128)}) fusion(bf16[8,1,393216]{2,1,0:T(2,128)(2,1)} %reshape.505), kind=kLoop, calls=%fused_computation.26 | loop fusion | flops 3145728 | bytes 18874368 | tf_op jit(solution)/shard_map/convert_element_type | solution.py:19
  518.2 9.8 %reshape.321 = f32[3,2048,256]{2,1,0:T(8,128)} reshape(f32[4,393216]{1,0:T(4,128)} %get-tuple-element.5) | data formatting | bytes 12582912 | tf_op jit(solution)/shard_map/convert_element_type | solution.py:24
  527.9 22.2 %multiply_reduce_fusion = f32[8,196608]{1,0:T(8,128)} fusion(f32[8,1,196608]{2,1,0:T(1,128)} %all-to-all-done.6), kind=kLoop, calls=%fused_computation.38 | loop fusion | flops 1572864 | bytes 12582912 | tf_op jit(solution)/shard_map/mul | solution.py:21
  550.1 6.4 mul.189
  556.5 9.7 %reshape.322 = f32[3,2048,256]{2,1,0:T(8,128)} reshape(f32[4,393216]{1,0:T(4,128)} %get-tuple-element.4) | data formatting | bytes 12582912 | tf_op jit(solution)/shard_map/convert_element_type | solution.py:19
  566.2 22.0 %multiply_reduce_fusion.1 = f32[8,196608]{1,0:T(8,128)} fusion(f32[8,1,196608]{2,1,0:T(1,128)} %all-to-all-done.4), kind=kLoop, calls=%fused_computation.39 | loop fusion | flops 1572864 | bytes 12582912 | tf_op jit(solution)/shard_map/mul | solution.py:20
  588.3 6.4 mul.182
  594.7 12.1 %fusion.11 = bf16[3,2048,256]{2,1,0:T(8,128)(2,1)} fusion(f32[3,2048,256]{2,1,0:T(8,128)} %reshape.321, f32[3,2048,256]{2,1,0:T(8,128)} %mul.189, f32[3,2048,256]{2,1,0:T(8,128)} %reshape.322, f32[3,2048,256]{2,1,0:T(8,128)} %mul.182), kind=kLoop, calls=%fused_computation.40 | loop fusion | flops 17301504 | bytes 28311552 | tf_op jit(solution)/shard_map/convert_element_type | solution.py:25
  624.3 36.2 %all_to_all.64 = bf16[8,80,2048]{2,1,0:T(8,128)(2,1)} all-to-all(bf16[8,80,2048]{2,1,0:T(8,128)(2,1)S(1)} %broadcast_select_fusion), channel_id=1, replica_groups=mesh['dp'=8,'expert'=4] {'dp'}, dimensions={0} | all-to-all | bytes 5242880 | tf_op jit(solution)/shard_map/all_to_all | solution.py:98
  660.5 166.6 %all-gather.2.cloned.1.call-done = bf16[3,2048,1024]{2,1,0:T(8,128)(2,1)} async-done(((bf16[3,2048,256]{2,1,0:T(8,128)(2,1)}), bf16[3,2048,1024]{2,1,0:T(8,128)(2,1)}) %all-gather.2.cloned.1.call-update) | async-done | bytes 12582928 | tf_op jit(solution)/shard_map/all_gather | solution.py:103
  827.0 7.3 fusion.13
  834.4 12.6 %multiply_convert_fusion = bf16[640,2048]{1,0:T(8,128)(2,1)} fusion(bf16[3,2048,1024]{2,1,0:T(8,128)(2,1)} %all-gather.2.cloned.1.call-done, f32[640,1024]{1,0:T(8,128)} %fusion.13, bf16[640,2048]{1,0:T(8,128)(2,1)} %bitcast.76), kind=kOutput, calls=%fused_computation.41 | convolution fusion | flops 5376573440 | bytes 16252928 | tf_op jit(solution)/shard_map/dot_general | solution.py:107
  852.1 9.8 %reshape.324 = f32[1,3,2048,256]{3,2,1,0:T(8,128)} reshape(f32[4,393216]{1,0:T(4,128)} %get-tuple-element.5) | data formatting | bytes 12582912 | tf_op jit(solution)/shard_map/convert_element_type | solution.py:24
  861.9 6.4 mul.201
  868.3 9.8 %reshape.325 = f32[1,3,2048,256]{3,2,1,0:T(8,128)} reshape(f32[4,393216]{1,0:T(4,128)} %get-tuple-element.4) | data formatting | bytes 12582912 | tf_op jit(solution)/shard_map/convert_element_type | solution.py:19
  878.1 6.4 mul.206
  884.5 14.5 %subtract_convert_fusion = (bf16[1,3,2048,256]{3,2,1,0:T(8,128)(2,1)}, f32[1,3,2048,256]{3,2,1,0:T(8,128)}, f32[1,3,2048,256]{3,2,1,0:T(8,128)}) fusion(f32[1,3,2048,256]{3,2,1,0:T(8,128)} %reshape.324, f32[1,3,2048,256]{3,2,1,0:T(8,128)} %mul.201, f32[1,3,2048,256]{3,2,1,0:T(8,128)} %reshape.325, f32[1,3,2048,256]{3,2,1,0:T(8,128)} %mul.206), kind=kLoop, calls=%fused_computation.36 | loop fusion | flops 17301504 | bytes 40894464 | tf_op jit(solution)/shard_map/convert_element_type | solution.py:25
  899.0 6.5 gather_fusion.2
  909.5 9.9 %multiply_reduce_fusion.2 = bf16[256,2048]{1,0:T(8,128)(2,1)} fusion(f32[256,2,2048]{2,1,0:T(2,128)} %reshape.323, f32[256,2]{1,0:T(8,128)S(1)} %copy.25), kind=kLoop, calls=%fused_computation.48 | loop fusion | flops 1572864 | bytes 5244928 | tf_op jit(solution)/shard_map/reduce_sum | solution.py:119
  (69 shorter events, 78.3 us)
Async XLA Ops:
  7.2 610.9 %copy-start = (bf16[256,2048]{1,0:T(8,128)(2,1)S(1)}, bf16[256,2048]{1,0:T(8,128)(2,1)}, u32[]{:S(2)}) copy-start(bf16[256,2048]{1,0:T(8,128)(2,1)} %param.9) | copy-start | bytes 3145732
  75.0 77.0 %all-to-all-start.1 = ((bf16[8,2,196608]{2,1,0:T(2,128)(2,1)}), bf16[8,2,196608]{2,1,0:T(2,128)(2,1)}, u32[]{:S(2)}, u32[]{:S(2)}) async-start(bf16[8,2,196608]{2,1,0:T(2,128)(2,1)} %reshape.502), calls=%async_computation.1 | async-start | bytes 12582912 | tf_op jit(solution)/shard_map/all_to_all | solution.py:36
  90.6 10.6 %copy-start.6 = (s32[8]{0:T(128)S(1)}, s32[8]{0:T(128)}, u32[]{:S(2)}) copy-start(s32[8]{0:T(128)} %param.12) | copy-start | bytes 100
  90.6 21.1 %copy-start.7 = (s32[8]{0:T(128)S(1)}, s32[8]{0:T(128)}, u32[]{:S(2)}) copy-start(s32[8]{0:T(128)} %param.13) | copy-start | bytes 100
  111.7 0.6 copy-start.5
  152.0 76.4 %all-to-all-start.5 = ((f32[8,1,196608]{2,1,0:T(1,128)}), f32[8,1,196608]{2,1,0:T(1,128)}, u32[]{:S(2)}, u32[]{:S(2)}) async-start(f32[8,1,196608]{2,1,0:T(1,128)} %all_to_all.50), calls=%async_computation.5 | async-start | bytes 12582912 | tf_op jit(solution)/shard_map/all_to_all | solution.py:46
  228.4 76.4 %all-to-all-start.3 = ((f32[8,1,196608]{2,1,0:T(1,128)}), f32[8,1,196608]{2,1,0:T(1,128)}, u32[]{:S(2)}, u32[]{:S(2)}) async-start(f32[8,1,196608]{2,1,0:T(1,128)} %all_to_all.45), calls=%async_computation.3 | async-start | bytes 12582912 | tf_op jit(solution)/shard_map/all_to_all | solution.py:43
  304.8 76.6 %all-to-all-start.2 = ((bf16[8,2,196608]{2,1,0:T(2,128)(2,1)}), bf16[8,2,196608]{2,1,0:T(2,128)(2,1)}, u32[]{:S(2)}, u32[]{:S(2)}) async-start(bf16[8,2,196608]{2,1,0:T(2,128)(2,1)} %reshape.504), calls=%async_computation.2 | async-start | bytes 12582912 | tf_op jit(solution)/shard_map/all_to_all | solution.py:51
  316.6 3.6 copy-start.1
  316.6 5.1 copy-start.2
  381.4 76.6 %all-to-all-start.6 = ((f32[8,1,196608]{2,1,0:T(1,128)}), f32[8,1,196608]{2,1,0:T(1,128)}, u32[]{:S(2)}, u32[]{:S(2)}) async-start(f32[8,1,196608]{2,1,0:T(1,128)} %copy.24), calls=%async_computation.6 | async-start | bytes 12582912 | tf_op jit(solution)/shard_map/all_to_all | solution.py:55
  458.0 108.3 %all-to-all-start.4 = ((f32[8,1,196608]{2,1,0:T(1,128)}), f32[8,1,196608]{2,1,0:T(1,128)}, u32[]{:S(2)}, u32[]{:S(2)}) async-start(f32[8,1,196608]{2,1,0:T(1,128)} %copy.23), calls=%async_computation.4 | async-start | bytes 12582912 | tf_op jit(solution)/shard_map/all_to_all | solution.py:54
  462.8 364.3 %all-gather.2.cloned.1.call-start = ((), (), s32[]{:S(2)}) async-start(), calls=%async_computation.8 | async-start | bytes 15728640 | tf_op jit(solution)/shard_map/all_gather | solution.py:103
  594.7 12.1 %copy-start.3 = (s32[256,2]{0,1:T(2,128)S(1)}, s32[256,2]{0,1:T(2,128)}, u32[]{:S(2)}) copy-start(s32[256,2]{0,1:T(2,128)} %param.10) | copy-start | bytes 6148
  847.0 5.0 copy-start.4
  847.0 52.0 %all-to-all-start.7 = ((bf16[8,80,2048]{2,1,0:T(8,128)(2,1)}), bf16[8,80,2048]{2,1,0:T(8,128)(2,1)}, u32[]{:S(2)}, u32[]{:S(2)}) async-start(bf16[8,80,2048]{2,1,0:T(8,128)(2,1)} %bitcast.74), calls=%async_computation.7 | async-start | bytes 5242880 | tf_op jit(solution)/shard_map/all_to_all | solution.py:111
Sparse Core Ops, SparseCore 0:
  606.9 220.0 all-gather.1
where the time goes:
time: 937 us; the launch traced here: 926 us
  waiting for transfers between devices  333 us (36%)
  local copies, waits for them, and re-layouts  281 us (30%)
  other arithmetic  208 us (22%)
  blocking collectives  36.2 us (4%)
  starting transfers between devices  34.5 us (4%)
  matrix products  20 us (2%)
  between operations  14.5 us (2%)
    all_gather x1, waiting for transfers between devices, local(): columns = lax.all_gather(new_params[0], 'expert', axis=2, tiled=True)  167 us
    unnamed x24, local copies, waits for them, and re-layouts  60.8 us
    all_to_all x1, waiting for transfers between devices, relocate(): lax.all_to_all(spread[2][source], 'dp', split_axis=0, concat_axis=0, tile...  53.9 us
    convert_element_type x2, other arithmetic, relocate(): leading.reshape(pieces, -1).astype(jnp.float32)  46.4 us
    convert_element_type x1, other arithmetic, adam_update(): grad_value = grads.astype(jnp.float32)  44.4 us
    all_to_all x1, waiting for transfers between devices, relocate(): lax.all_to_all(leading.reshape(pieces, -1).astype(jnp.float32), 'dp', spl...  39.1 us
    all_to_all x1, blocking collectives, local(): lax.all_to_all(outgoing.reshape(experts, capacity, features), 'dp', split...  36.2 us
    all_to_all x1, waiting for transfers between devices, relocate(): lax.all_to_all(spread[0][source].astype(jnp.float32), 'dp', split_axis=0,...  29.4 us
  transfers between devices with their start and end apart: 8, of which 6 were waited for; matrix products, arithmetic and copies ran while one was open for 36% of the time, Pallas kernels for 0%

commit v1 on v0

--- a/solution.py
+++ b/solution.py
@@ -30,30 +30,20 @@
     return jnp.zeros((entries,), jnp.int32).at[placement].set(jnp.arange(entries, dtype=jnp.int32))
 
 
-def relocate(leading, first_moment, second_moment, source):
+def spread_blocks(value):
     pieces = lax.axis_size("dp")
-    spread = (
-        lax.all_to_all(
-            leading.reshape(pieces, -1).astype(jnp.float32),
-            "dp",
-            split_axis=0,
-            concat_axis=0,
-            tiled=True,
-        ).astype(jnp.bfloat16),
-        lax.all_to_all(
-            first_moment.reshape(pieces, -1), "dp", split_axis=0, concat_axis=0, tiled=True
-        ),
-        lax.all_to_all(
-            second_moment.reshape(pieces, -1), "dp", split_axis=0, concat_axis=0, tiled=True
-        ),
-    )
-    return (
-        lax.all_to_all(
-            spread[0][source].astype(jnp.float32), "dp", split_axis=0, concat_axis=0, tiled=True
-        ).astype(jnp.bfloat16),
-        lax.all_to_all(spread[1][source], "dp", split_axis=0, concat_axis=0, tiled=True),
-        lax.all_to_all(spread[2][source], "dp", split_axis=0, concat_axis=0, tiled=True),
-    )
+    kinds, depth, width = value.shape
+    return value.reshape(kinds, pieces, depth // pieces, width).transpose(1, 0, 2, 3)
+
+
+def joined_blocks(blocks):
+    pieces, kinds, depth, width = blocks.shape
+    return blocks.transpose(1, 0, 2, 3).reshape(kinds, pieces * depth, width)
+
+
+def relocate(blocks, source):
+    spread = lax.all_to_all(blocks, "dp", split_axis=0, concat_axis=0, tiled=True)
+    return lax.all_to_all(spread[source], "dp", split_axis=0, concat_axis=0, tiled=True)
 
 
 def local(
@@ -72,15 +62,22 @@
     topk = expert_ids.shape[1]
     capacity = 5 * tok_rows * topk // (4 * experts)
     source = inverse_of(old_place)[new_place]
-    leading = jnp.stack([params, grads])
-    delivered = relocate(leading, first_moment, second_moment, source)
-    weight_pair = delivered[0].reshape((2,) + params.shape)
-    new_params, new_first, new_second = adam_update(
-        weight_pair[0],
-        weight_pair[1],
-        delivered[1].reshape(first_moment.shape),
-        delivered[2].reshape(second_moment.shape),
+    own_params, own_first, own_second = adam_update(
+        params[0], grads[0], first_moment[0], second_moment[0]
     )
+    moved_params = relocate(spread_blocks(own_params), source)
+    moments = jnp.concatenate(
+        [
+            spread_blocks(own_first.astype(jnp.bfloat16)),
+            spread_blocks(own_second.astype(jnp.bfloat16)),
+        ],
+        axis=1,
+    )
+    moved_moments = relocate(moments, source)
+    new_params = joined_blocks(moved_params)[None]
+    kinds = params.shape[1]
+    new_first = joined_blocks(moved_moments[:, :kinds]).astype(jnp.float32)[None]
+    new_second = joined_blocks(moved_moments[:, kinds:]).astype(jnp.float32)[None]
     flat_ids = expert_ids.reshape(-1)
     onehot = (flat_ids[:, None] == jnp.arange(experts, dtype=jnp.int32)[None, :]).astype(jnp.int32)
     slot_rank = jnp.sum((jnp.cumsum(onehot, axis=0) - 1) * onehot, axis=1)

time: 937 us -> 413 us (0.44); the launches traced: 926 us -> 412 us
  local copies, waits for them, and re-layouts: 281 us -> 41.8 us
  other arithmetic: 208 us -> 42.9 us
  waiting for transfers between devices: 333 us -> 230 us
  starting transfers between devices: 34.5 us -> 23 us
    convert_element_type x7 -> x1, other arithmetic: 138 us -> 4.49 us  [local(): joined_blocks(moved_moments[:, kinds:]).astype(jnp.float32)[None]]
    all_gather x1, waiting for transfers between devices: 167 us -> 94.3 us  [local(): columns = lax.all_gather(new_params[0], 'expert', axis=2, tiled=True)]
    all_to_all x5 -> x0, local copies, waits for them, and re-layouts: 61.1 us -> none  [the longest x1 14.1 us: relocate(): lax.all_to_all(spread[1][source], 'dp', split_axis=0, concat_axis=0, tile...]
    unnamed x24 -> x20, local copies, waits for them, and re-layouts: 60.8 us -> 3.67 us
    all_to_all x6 -> x4, waiting for transfers between devices: 166 us -> 115 us  [the longest x2 89.6 us: relocate(): lax.all_to_all(blocks, 'dp', split_axis=0, concat_axis=0, tiled=True)]
    gather x11 -> x2, local copies, waits for them, and re-layouts: 53.7 us -> 10.8 us  [relocate(): spread[source]]
    convert_element_type x6 -> x2, local copies, waits for them, and re-layouts: 49 us -> 6.71 us  [the longest x1 3.36 us: local(): joined_blocks(moved_moments[:, :kinds]).astype(jnp.float32)[None]]
    mul x4 -> x0, local copies, waits for them, and re-layouts: 25.6 us -> none  [the longest x2 12.8 us: adam_update(): new_first = first_decay * first_moment + (1.0 - first_decay) * grad_value]
  transfers between devices with their start and end apart: 8 -> 6, of which waited for: 6 -> 5; matrix products, arithmetic and copies ran while one was open for 36% -> 15% of each run, Pallas kernels for 0% -> 0%
where the time goes in v1:
time: 413 us; the launch traced here: 412 us
  waiting for transfers between devices  230 us (56%)
  other arithmetic  42.9 us (10%)
  local copies, waits for them, and re-layouts  41.8 us (10%)
  blocking collectives  41.4 us (10%)
  starting transfers between devices  23 us (6%)
  matrix products  18.3 us (4%)
  between operations  14.3 us (3%)
    all_gather x1, waiting for transfers between devices, local(): columns = lax.all_gather(new_params[0], 'expert', axis=2, tiled=True)  94.3 us
    all_to_all x2, waiting for transfers between devices, relocate(): lax.all_to_all(blocks, 'dp', split_axis=0, concat_axis=0, tiled=True)  89.6 us
    all_to_all x1, blocking collectives, relocate(): lax.all_to_all(spread[source], 'dp', split_axis=0, concat_axis=0, tiled=T...  41.4 us
    all_to_all x1, waiting for transfers between devices, local(): lax.all_to_all(outgoing.reshape(experts, capacity, features), 'dp', split...  25.7 us
    all_to_all x1, waiting for transfers between devices, local(): lax.all_to_all(expert_out.reshape(experts, capacity, features), 'dp', spl...  20.7 us
    dot_general x1, matrix products, local(): lax.dot_general(hidden, columns[2], (((1,), (1,)), ((), ())), preferred_e...  11.8 us
    gather x2, local copies, waits for them, and re-layouts, relocate(): spread[source]  10.8 us
    all_to_all x2, starting transfers between devices, relocate(): lax.all_to_all(blocks, 'dp', split_axis=0, concat_axis=0, tiled=True)  10.3 us
  transfers between devices with their start and end apart: 6, of which 5 were waited for; matrix products, arithmetic and copies ran while one was open for 15% of the time, Pallas kernels for 0%

profile of v1, /device:TPU:0, one launch (start us, length us, event | category | flops | bytes accessed | tf_op | source)
XLA Modules:
  0.0 412.0 jit_solution(14918557196728392944)
XLA Ops:
  7.2 3.6 broadcast_multiply_fusion.1
  10.8 1.1 copy-done.2
  11.9 0.5 broadcast_multiply_fusion
  12.4 1.3 copy-done.3
  13.8 1.0 copy-done.4
  14.7 8.5 %convert_bitcast_fusion.3 = (bf16[8,3,256,256]{3,2,1,0:T(8,128)(2,1)}, bf16[8,3,256,256]{3,2,1,0:T(8,128)(2,1)}, bf16[8,3,256,256]{3,2,1,0:T(8,128)(2,1)}) fusion(f32[3,8,256,256]{3,2,1,0:T(8,128)S(1)} %bitcast.64, f32[3,8,256,256]{3,2,1,0:T(8,128)S(1)} %bitcast.65, bf16[3,8,256,256]{3,2,1,0:T(8,128)(2,1)S(1)} %bitcast.72, ...), kind=kLoop, calls=%fused_computation.25 | loop fusion | flops 23592960 | bytes 28311552 | tf_op jit(solution)/shard_map/transpose | solution.py:36
  23.2 5.3 %all-to-all-start.1 = ((bf16[8,3,256,256]{3,2,1,0:T(8,128)(2,1)}), bf16[8,3,256,256]{3,2,1,0:T(8,128)(2,1)}, u32[]{:S(2)}, u32[]{:S(2)}) async-start(bf16[8,3,256,256]{3,2,1,0:T(8,128)(2,1)} %get-tuple-element.5), calls=%async_computation.1 | async-start | bytes 6291456 | tf_op jit(solution)/shard_map/all_to_all | solution.py:45
  28.5 0.0 all-gather.2.cloned.1.call-start
  28.6 0.6 scatter_custom_fusion.2
  29.2 0.6 gather_fusion.1
  29.9 36.6 %all-to-all-done.1 = bf16[8,3,256,256]{3,2,1,0:T(8,128)(2,1)} async-done(((bf16[8,3,256,256]{3,2,1,0:T(8,128)(2,1)}), bf16[8,3,256,256]{3,2,1,0:T(8,128)(2,1)}, u32[]{:S(2)}, u32[]{:S(2)}) %all-to-all-start.1) | async-done | bytes 3145760 | tf_op jit(solution)/shard_map/all_to_all | solution.py:45
  66.5 4.3 %gather_fusion.2 = bf16[8,3,256,256]{3,2,1,0:T(8,128)(2,1)} fusion(bf16[8,3,256,256]{3,2,1,0:T(8,128)(2,1)} %all-to-all-done.1, s32[1024]{0:T(1024)S(1)} %pad_clamp_fusion.1), kind=kCustom, calls=%fused_computation.2 | custom fusion | bytes 6291488 | tf_op jit(solution)/shard_map/gather | solution.py:46
  70.8 41.4 %all_to_all.30 = bf16[8,3,256,256]{3,2,1,0:T(8,128)(2,1)S(1)} all-to-all(bf16[8,3,256,256]{3,2,1,0:T(8,128)(2,1)} %gather_fusion.2), channel_id=1, replica_groups=mesh['dp'=8,'expert'=4] {'dp'}, dimensions={0} | all-to-all | bytes 6291456 | tf_op jit(solution)/shard_map/all_to_all | solution.py:46
  112.2 2.0 copy.27
  114.2 6.1 %pad_maximum_fusion = bf16[8,6,256,256]{3,2,1,0:T(8,128)(2,1)} fusion(bf16[8,3,256,256]{3,2,1,0:T(8,128)(2,1)} %get-tuple-element.6, bf16[8,3,256,256]{3,2,1,0:T(8,128)(2,1)} %get-tuple-element.4), kind=kLoop, calls=%fused_computation.10 | loop fusion | flops 3145728 | bytes 12582912 | tf_op jit(solution)/shard_map/concatenate | solution.py:69
  120.3 5.0 %all-to-all-start.4 = ((bf16[8,6,256,256]{3,2,1,0:T(8,128)(2,1)}), bf16[8,6,256,256]{3,2,1,0:T(8,128)(2,1)}, u32[]{:S(2)}, u32[]{:S(2)}) async-start(bf16[8,6,256,256]{3,2,1,0:T(8,128)(2,1)} %pad_maximum_fusion), calls=%async_computation.4 | async-start | bytes 12582912 | tf_op jit(solution)/shard_map/all_to_all | solution.py:45
  125.4 0.1 copy.18
  125.5 0.1 reshape.164
  125.6 0.1 eq.29
  125.8 0.1 eq.25
  125.9 0.6 scatter_custom_fusion
  126.6 1.1 reduce-window.6
  127.7 0.2 slice_reduce_fusion
  128.0 0.7 fusion.23
  128.7 0.1 fusion.8
  128.8 4.3 %compare_select_fusion.2 = s32[512,1]{0,1:T(1,128)S(1)} fusion(s32[]{:T(128)} %bitcast.1, s32[]{:T(128)} %bitcast.2, s32[]{:T(128)} %bitcast.3, s32[]{:T(128)} %bitcast.4, s32[]{:T(128)} %bitcast.5, s32[]{:T(128)} %bitcast.7, s32[]{:T(128)} %bitcast.6, s32[512,1]{0,1:T(1,128)S(1)} %reshape.164), kind=kLoop, calls=%fused_computation.42 | loop fusion | flops 7680 | bytes 4124 | tf_op jit(solution)/shard_map/gather | solution.py:84
  133.1 0.7 fusion.12
  133.7 2.4 scatter_custom_fusion.1
  136.2 0.1 broadcast_in_dim.39
  136.3 4.1 gather_fusion
  140.4 3.5 broadcast_select_fusion
  143.9 53.0 %all-to-all-done.4 = bf16[8,6,256,256]{3,2,1,0:T(8,128)(2,1)} async-done(((bf16[8,6,256,256]{3,2,1,0:T(8,128)(2,1)}), bf16[8,6,256,256]{3,2,1,0:T(8,128)(2,1)}, u32[]{:S(2)}, u32[]{:S(2)}) %all-to-all-start.4) | async-done | bytes 6291488 | tf_op jit(solution)/shard_map/all_to_all | solution.py:45
  196.9 3.6 all-to-all-start
  200.6 6.5 %gather_fusion.4 = bf16[8,6,256,256]{3,2,1,0:T(8,128)(2,1)} fusion(bf16[8,6,256,256]{3,2,1,0:T(8,128)(2,1)} %all-to-all-done.4, s32[1024]{0:T(1024)S(1)} %pad_clamp_fusion.1), kind=kCustom, calls=%fused_computation.4 | custom fusion | bytes 12582944 | tf_op jit(solution)/shard_map/gather | solution.py:46
  207.1 25.7 %all-to-all-done = bf16[8,80,2048]{2,1,0:T(8,128)(2,1)S(1)} async-done(((bf16[8,80,2048]{2,1,0:T(8,128)(2,1)}), bf16[8,80,2048]{2,1,0:T(8,128)(2,1)S(1)}, u32[]{:S(2)}, u32[]{:S(2)}) %all-to-all-start) | async-done | bytes 2621472 | tf_op jit(solution)/shard_map/all_to_all | solution.py:95
  232.8 5.0 %all-to-all-start.5 = ((bf16[8,6,256,256]{3,2,1,0:T(8,128)(2,1)}), bf16[8,6,256,256]{3,2,1,0:T(8,128)(2,1)}, u32[]{:S(2)}, u32[]{:S(2)}) async-start(bf16[8,6,256,256]{3,2,1,0:T(8,128)(2,1)} %gather_fusion.4), calls=%async_computation.5 | async-start | bytes 12582912 | tf_op jit(solution)/shard_map/all_to_all | solution.py:46
  237.8 94.3 %all-gather.2.cloned.1.call-done = bf16[3,2048,1024]{2,1,0:T(8,128)(2,1)} async-done(((bf16[3,2048,256]{2,1,0:T(8,128)(2,1)}), bf16[3,2048,1024]{2,1,0:T(8,128)(2,1)}) %all-gather.2.cloned.1.call-update) | async-done | bytes 12582928 | tf_op jit(solution)/shard_map/all_gather | solution.py:100
  332.1 6.5 %fusion.3 = f32[640,1024]{1,0:T(8,128)} fusion(bf16[640,2048]{1,0:T(8,128)(2,1)S(1)} %bitcast.75, bf16[3,2048,1024]{2,1,0:T(8,128)(2,1)} %all-gather.2.cloned.1.call-done), kind=kOutput, calls=%fused_computation.20 | convolution fusion | flops 2684354560 | bytes 9437184 | tf_op jit(solution)/shard_map/dot_general | solution.py:102
  338.6 11.8 %multiply_convert_fusion = bf16[640,2048]{1,0:T(8,128)(2,1)} fusion(bf16[3,2048,1024]{2,1,0:T(8,128)(2,1)} %all-gather.2.cloned.1.call-done, f32[640,1024]{1,0:T(8,128)} %fusion.3, bf16[640,2048]{1,0:T(8,128)(2,1)S(1)} %bitcast.76), kind=kOutput, calls=%fused_computation.16 | convolution fusion | flops 5376573440 | bytes 16252928 | tf_op jit(solution)/shard_map/dot_general | solution.py:104
  350.4 4.0 all-to-all-start.3
  354.4 0.1 copy.28
  354.6 4.5 %convert_bitcast_fusion = (f32[3,8,256,256]{3,2,0,1:T(8,128)S(1)}, f32[3,8,256,256]{3,2,0,1:T(8,128)S(1)}) fusion(bf16[8,6,256,256]{3,2,1,0:T(8,128)(2,1)} %all-to-all-done.5), kind=kLoop, calls=%fused_computation.14 | loop fusion | flops 3145728 | bytes 18874368 | tf_op jit(solution)/shard_map/convert_element_type | solution.py:80
  359.1 3.4 copy.30
  362.4 3.4 copy.31
  365.8 20.7 %all-to-all-done.3 = bf16[8,80,2048]{2,1,0:T(8,128)(2,1)S(1)} async-done(((bf16[8,80,2048]{2,1,0:T(8,128)(2,1)}), bf16[8,80,2048]{2,1,0:T(8,128)(2,1)S(1)}, u32[]{:S(2)}, u32[]{:S(2)}) %all-to-all-start.3) | async-done | bytes 2621472 | tf_op jit(solution)/shard_map/all_to_all | solution.py:108
  386.4 3.3 gather_fusion.3
  389.8 5.5 %reshape.171 = f32[256,2,2048]{2,1,0:T(2,128)} reshape(bf16[512,2048]{1,0:T(8,128)(2,1)} %gather_fusion.3) | data formatting | bytes 6291456 | tf_op jit(solution)/shard_map/convert_element_type | solution.py:115
  395.3 9.9 %multiply_reduce_fusion = bf16[256,2048]{1,0:T(8,128)(2,1)} fusion(f32[256,2,2048]{2,1,0:T(2,128)} %reshape.171, f32[256,2]{1,0:T(8,128)S(1)} %copy.28), kind=kLoop, calls=%fused_computation.23 | loop fusion | flops 1572864 | bytes 5244928 | tf_op jit(solution)/shard_map/reduce_sum | solution.py:116
  (34 shorter events, 0.2 us)
Async XLA Ops:
  7.2 129.2 %copy-start = (bf16[256,2048]{1,0:T(8,128)(2,1)S(1)}, bf16[256,2048]{1,0:T(8,128)(2,1)}, u32[]{:S(2)}) copy-start(bf16[256,2048]{1,0:T(8,128)(2,1)} %param.9) | copy-start | bytes 3145732
  7.2 4.7 %copy-start.2 = (f32[1,3,2048,256]{3,2,1,0:T(8,128)S(1)}, f32[1,3,2048,256]{3,2,1,0:T(8,128)}, u32[]{:S(2)}) copy-start(f32[1,3,2048,256]{3,2,1,0:T(8,128)} %param.17) | copy-start | bytes 18874372
  11.9 1.9 copy-start.3
  11.9 2.8 copy-start.4
  23.2 5.4 %copy-start.7 = (s32[8]{0:T(128)S(1)}, s32[8]{0:T(128)}, u32[]{:S(2)}) copy-start(s32[8]{0:T(128)} %param.12) | copy-start | bytes 100
  23.2 6.0 %copy-start.8 = (s32[8]{0:T(128)S(1)}, s32[8]{0:T(128)}, u32[]{:S(2)}) copy-start(s32[8]{0:T(128)} %param.13) | copy-start | bytes 100
  23.2 43.3 %all-to-all-start.1 = ((bf16[8,3,256,256]{3,2,1,0:T(8,128)(2,1)}), bf16[8,3,256,256]{3,2,1,0:T(8,128)(2,1)}, u32[]{:S(2)}, u32[]{:S(2)}) async-start(bf16[8,3,256,256]{3,2,1,0:T(8,128)(2,1)} %get-tuple-element.5), calls=%async_computation.1 | async-start | bytes 6291456 | tf_op jit(solution)/shard_map/all_to_all | solution.py:45
  28.5 303.5 %all-gather.2.cloned.1.call-start = ((), (), s32[]{:S(2)}) async-start(), calls=%async_computation.6 | async-start | bytes 15728640 | tf_op jit(solution)/shard_map/all_gather | solution.py:100
  120.3 5.1 %copy-start.5 = (s32[256,2]{0,1:T(2,128)S(1)}, s32[256,2]{0,1:T(2,128)}, u32[]{:S(2)}) copy-start(s32[256,2]{0,1:T(2,128)} %param.10) | copy-start | bytes 6148
  120.3 76.6 %all-to-all-start.4 = ((bf16[8,6,256,256]{3,2,1,0:T(8,128)(2,1)}), bf16[8,6,256,256]{3,2,1,0:T(8,128)(2,1)}, u32[]{:S(2)}, u32[]{:S(2)}) async-start(bf16[8,6,256,256]{3,2,1,0:T(8,128)(2,1)} %pad_maximum_fusion), calls=%async_computation.4 | async-start | bytes 12582912 | tf_op jit(solution)/shard_map/all_to_all | solution.py:45
  196.9 35.8 %all-to-all-start = ((bf16[8,80,2048]{2,1,0:T(8,128)(2,1)}), bf16[8,80,2048]{2,1,0:T(8,128)(2,1)S(1)}, u32[]{:S(2)}, u32[]{:S(2)}) async-start(bf16[8,80,2048]{2,1,0:T(8,128)(2,1)} %broadcast_select_fusion), calls=%async_computation | async-start | bytes 5242880 | tf_op jit(solution)/shard_map/all_to_all | solution.py:95
  232.8 117.6 %all-to-all-start.5 = ((bf16[8,6,256,256]{3,2,1,0:T(8,128)(2,1)}), bf16[8,6,256,256]{3,2,1,0:T(8,128)(2,1)}, u32[]{:S(2)}, u32[]{:S(2)}) async-start(bf16[8,6,256,256]{3,2,1,0:T(8,128)(2,1)} %gather_fusion.4), calls=%async_computation.5 | async-start | bytes 12582912 | tf_op jit(solution)/shard_map/all_to_all | solution.py:46
  350.4 4.0 copy-start.6
  350.4 36.0 %all-to-all-start.3 = ((bf16[8,80,2048]{2,1,0:T(8,128)(2,1)}), bf16[8,80,2048]{2,1,0:T(8,128)(2,1)S(1)}, u32[]{:S(2)}, u32[]{:S(2)}) async-start(bf16[8,80,2048]{2,1,0:T(8,128)(2,1)} %bitcast.74), calls=%async_computation.3 | async-start | bytes 5242880 | tf_op jit(solution)/shard_map/all_to_all | solution.py:108
  389.8 15.4 %copy-start.1 = (bf16[256,2048]{1,0:T(8,128)(2,1)S(1)}, bf16[256,2048]{1,0:T(8,128)(2,1)}, u32[]{:S(2)}) copy-start(bf16[256,2048]{1,0:T(8,128)(2,1)} %param.9) | copy-start | bytes 3145732
Sparse Core Ops, SparseCore 0:
  114.3 217.6 all-gather.1

commit v2 on v1

v2 whole, which is shorter than its diff:
```python
import functools
import math

import jax
import jax.numpy as jnp
from jax import lax
from jax.experimental import pallas as pl
from jax.experimental.pallas import tpu as pltpu
from jax.sharding import PartitionSpec as P

adam_rate = 0.3
first_decay = 0.9
second_decay = 0.95
adam_count = 10.0
adam_eps = 1e-08


def adam_update(params, grads, first_moment, second_moment):
    grad_value = grads.astype(jnp.float32)
    new_first = first_decay * first_moment + (1.0 - first_decay) * grad_value
    new_second = second_decay * second_moment + (1.0 - second_decay) * grad_value * grad_value
    first_hat = new_first / (1.0 - first_decay**adam_count)
    second_hat = new_second / (1.0 - second_decay**adam_count)
    stepped = params.astype(jnp.float32) - adam_rate * first_hat / (jnp.sqrt(second_hat) + adam_eps)
    return (stepped.astype(jnp.bfloat16), new_first, new_second)


def inverse_of(placement):
    number = jnp.arange(placement.shape[0], dtype=jnp.int32)
    return jnp.sum(jnp.where(placement[:, None] == number[None, :], number[:, None], 0), axis=0)


def swap(blocks):
    return lax.all_to_all(blocks, "dp", split_axis=0, concat_axis=0, tiled=True)


def move_kernel(
    rows_dp,
    shards,
    kinds,
    source,
    params,
    first,
    second,
    outgoing,
    weights,
    new_first,
    new_second,
    arrived,
    *scratch,
):
    chunks = 3 * kinds
    caught, sorted_ = scratch[:chunks], scratch[chunks : 2 * chunks]
    (one_send, one_recv, two_send, two_recv, own_sem, tok_send, tok_recv, z_send, z_recv) = scratch[
        2 * chunks :
    ]
    me, z = lax.axis_index("dp"), lax.axis_index("expert")
    block = params.shape[1] // rows_dp
    has_left, has_right = z > 0, z < shards - 1

    def rows(row):
        return pl.ds(pl.multiple_of(row * block, block), block)

    def remote(src, dst, send, recv, target):
        return pltpu.make_async_remote_copy(
            src_ref=src,
            dst_ref=dst,
            send_sem=send,
            recv_sem=recv,
            device_id=target,
            device_id_type=pl.DeviceIdType.MESH,
        )

    def peers(body):
        def step(offset, carry):
            body(lax.rem(me + offset, rows_dp))
            return carry

        lax.fori_loop(1, rows_dp, step, 0)

    def origin(chunk, row):
        return (params, first, second)[chunk // kinds].at[chunk % kinds, rows(row)]

    def final(chunk, row):
        if chunk < kinds:
            return weights.at[chunk, z, rows(row)]
        return (new_first, new_second)[chunk // kinds - 1].at[chunk % kinds, rows(row)]

    def one(chunk, peer, sender):
        return remote(
            origin(chunk, peer),
            caught[chunk].at[sender],
            one_send.at[chunk, peer],
            one_recv.at[chunk, sender],
            {"dp": peer},
        )

    def one_own(chunk):
        return pltpu.make_async_copy(
            origin(chunk, me), caught[chunk].at[me], own_sem.at[0, chunk]
        )

    def two(chunk, peer, sender):
        return remote(
            sorted_[chunk].at[peer],
            final(chunk, sender),
            two_send.at[chunk, peer],
            two_recv.at[chunk, sender],
            {"dp": peer},
        )

    def two_own(chunk):
        return pltpu.make_async_copy(
            sorted_[chunk].at[me], final(chunk, me), own_sem.at[1, chunk]
        )

    def tok(peer, sender):
        return remote(
            outgoing.at[peer],
            arrived.at[sender],
            tok_send.at[peer],
            tok_recv.at[sender],
            {"dp": peer},
        )

    def tok_own():
        return pltpu.make_async_copy(outgoing.at[me], arrived.at[me], tok_send.at[me])

    def along(kind, shard, way):
        return remote(
            weights.at[kind, shard],
            weights.at[kind, shard],
            z_send.at[kind, shard, way],
            z_recv.at[kind, shard],
            {"expert": z + (1 if way == 0 else -1)},
        )

    def start_one(chunk):
        one_own(chunk).start()
        peers(lambda peer: one(chunk, peer, me).start())

    def turn(chunk):
        one_own(chunk).wait()
        peers(lambda peer: one(chunk, peer, peer).wait_recv())

        def pick(row, carry):
            sorted_[chunk][row] = caught[chunk][source[row]]
            return carry

        lax.fori_loop(0, rows_dp, pick, 0)
        two_own(chunk).start()
        peers(lambda peer: two(chunk, peer, me).start())

    def finish_two(chunk):
        two_own(chunk).wait()
        peers(lambda peer: two(chunk, peer, peer).wait_recv())

    def z_own(kind):
        @pl.when(has_right)
        def _():
            along(kind, z, 0).start()

        @pl.when(has_left)
        def _():
            along(kind, z, 1).start()

    def z_step(kind, step):
        @pl.when(z - 1 - step >= 0)
        def _():
            along(kind, z - 1 - step, 0).wait_recv()

            @pl.when(has_right)
            def _():
                along(kind, z - 1 - step, 0).start()

        @pl.when(z + 1 + step < shards)
        def _():
            along(kind, z + 1 + step, 1).wait_recv()

            @pl.when(has_left)
            def _():
                along(kind, z + 1 + step, 1).start()

    def z_sent(kind, step):
        @pl.when(jnp.logical_and(z - step >= 0, has_right))
        def _():
            along(kind, z - step, 0).wait_send()

        @pl.when(jnp.logical_and(z + step < shards, has_left))
        def _():
            along(kind, z + step, 1).wait_send()

    barrier = pltpu.get_barrier_semaphore()

    def greet(target):
        pl.semaphore_signal(
            barrier, inc=1, device_id=target, device_id_type=pl.DeviceIdType.MESH
        )

    peers(lambda peer: greet({"dp": peer}))

    @pl.when(has_left)
    def _():
        greet({"expert": z - 1})

    @pl.when(has_right)
    def _():
        greet({"expert": z + 1})

    pl.semaphore_wait(
        barrier, rows_dp - 1 + has_left.astype(jnp.int32) + has_right.astype(jnp.int32)
    )

    started = 2
    for chunk in range(started):
        start_one(chunk)
    last = max(chunks + 1, kinds + 2 * shards)
    for tick in range(last):
        if tick < chunks:
            turn(tick)
        while started < min(chunks, tick + (3 if tick < kinds - 1 else 4)):
            start_one(started)
            started += 1
        if tick == kinds - 1:
            tok_own().start()
            peers(lambda peer: tok(peer, me).start())
        if 1 <= tick <= chunks:
            finish_two(tick - 1)
            if tick - 1 < kinds:
                z_own(tick - 1)
        for kind in range(kinds):
            step, odd = divmod(tick - kind - 2, 2)
            if odd == 0 and 0 <= step < shards - 1:
                z_step(kind, step)

    tok_own().wait()
    peers(lambda peer: tok(peer, peer).wait_recv())
    peers(lambda peer: tok(peer, me).wait_send())
    for chunk in range(chunks):
        peers(lambda peer: one(chunk, peer, me).wait_send())
        peers(lambda peer: two(chunk, peer, me).wait_send())
    for kind in range(kinds):
        for step in range(shards - 1):
            z_sent(kind, step)


def move(source, params, first, second, outgoing):
    kinds, depth, width = params.shape
    rows_dp, shards = lax.axis_size("dp"), lax.axis_size("expert")
    chunks = 3 * kinds
    held = pltpu.VMEM((rows_dp, depth // rows_dp, width), jnp.bfloat16)
    dma = pltpu.SemaphoreType.DMA
    state = jax.ShapeDtypeStruct(params.shape, jnp.bfloat16)
    anywhere = pl.BlockSpec(memory_space=pl.ANY)
    return pl.pallas_call(
        functools.partial(move_kernel, rows_dp, shards, kinds),
        out_shape=(
            jax.ShapeDtypeStruct((kinds, shards, depth, width), jnp.bfloat16),
            state,
            state,
            jax.ShapeDtypeStruct(outgoing.shape, jnp.bfloat16),
        ),
        in_specs=[pl.BlockSpec(memory_space=pltpu.SMEM)] + [anywhere] * 4,
        out_specs=(anywhere,) * 4,
        scratch_shapes=[held] * (2 * chunks)
        + [dma((chunks, rows_dp))] * 4
        + [
            dma((2, chunks)),
            dma((rows_dp,)),
            dma((rows_dp,)),
            dma((kinds, shards, 2)),
            dma((kinds, shards)),
        ],
        compiler_params=pltpu.CompilerParams(
            collective_id=0, has_side_effects=True, vmem_limit_bytes=44 * 1024 * 1024
        ),
    )(source, params, first, second, outgoing)


def local(
    tokens,
    expert_ids,
    gate_weights,
    old_place,
    new_place,
    params,
    grads,
    first_moment,
    second_moment,
):
    experts = old_place.shape[0]
    tok_rows, features = tokens.shape
    topk = expert_ids.shape[1]
    routes = tok_rows * topk
    capacity = 5 * routes // (4 * experts)
    slots = experts * capacity
    kinds, depth, width = params.shape[1:]
    shards = lax.axis_size("expert")
    half = features // 2
    source = inverse_of(old_place)[new_place]

    own_params, own_first, own_second = adam_update(
        params[0], grads[0], first_moment[0], second_moment[0]
    )

    flat_ids = expert_ids.reshape(-1)
    onehot = (flat_ids[:, None] == jnp.arange(experts, dtype=jnp.int32)[None, :])
    order = jnp.arange(routes, dtype=jnp.int32)
    earlier = (order[:, None] > order[None, :]).astype(jnp.bfloat16)
    counts = jnp.dot(earlier, onehot.astype(jnp.bfloat16), preferred_element_type=jnp.float32)
    slot_rank = jnp.sum(jnp.where(onehot, counts, 0.0), axis=1).astype(jnp.int32)
    row_of = inverse_of(new_place)
    route_row = jnp.sum(jnp.where(onehot, row_of[None, :], 0), axis=1)
    slot_index = (route_row * capacity + slot_rank).reshape(tok_rows, topk)
    slot_number = jnp.arange(slots, dtype=jnp.int32)
    hits = [slot_index[:, k, None] == slot_number[None, :] for k in range(topk)]
    chosen = sum(hit.astype(jnp.bfloat16) for hit in hits)
    mixing = sum(
        jnp.where(hits[k], gate_weights[:, k, None], 0.0) for k in range(topk)
    )
    mixing_high = mixing.astype(jnp.bfloat16)
    mixing_low = (mixing - mixing_high.astype(jnp.float32)).astype(jnp.bfloat16)

    outgoing = lax.dot_general(
        chosen, tokens, (((0,), (0,)), ((), ())), preferred_element_type=jnp.float32
    ).astype(jnp.bfloat16)
    weights, moved_first, moved_second, arrived = move(
        source,
        own_params,
        own_first.astype(jnp.bfloat16),
        own_second.astype(jnp.bfloat16),
        outgoing.reshape(experts, capacity, features),
    )
    arrived = arrived.reshape(slots, features)
    new_params = lax.dynamic_index_in_dim(
        weights, lax.axis_index("expert"), axis=1, keepdims=False
    )[None]
    new_first = moved_first.astype(jnp.float32)[None]
    new_second = moved_second.astype(jnp.float32)[None]

    in_scale = 1.0 / math.sqrt(features)
    out_scale = 1.0 / math.sqrt(width * shards)

    def into(kind):
        return [
            jnp.dot(arrived, weights[kind, z], preferred_element_type=jnp.float32) * in_scale
            for z in range(shards)
        ]

    gate_part, up_part = into(0), into(1)
    hidden = [
        (jax.nn.silu(gate) * up).astype(jnp.bfloat16) for gate, up in zip(gate_part, up_part)
    ]
    mixed = []
    for start in (0, half):
        summed = sum(
            lax.dot_general(
                hidden[z],
                weights[2, z, start : start + half],
                (((1,), (1,)), ((), ())),
                preferred_element_type=jnp.float32,
            )
            for z in range(shards)
        )
        expert_out = (summed * out_scale).astype(jnp.bfloat16)
        returned = swap(expert_out.reshape(experts, capacity, -1)).reshape(slots, -1)
        total = jnp.dot(mixing_high, returned, preferred_element_type=jnp.float32)
        total += jnp.dot(mixing_low, returned, preferred_element_type=jnp.float32)
        mixed.append(total.astype(jnp.bfloat16))
    return (jnp.concatenate(mixed, axis=1), new_params, new_first, new_second)


def solution(mesh):
    row, state = P(("dp", "expert"), None), P("dp", None, None, "expert")
    return jax.shard_map(
        local,
        mesh=mesh,
        in_specs=(row, row, row, P(), P(), state, state, state, state),
        out_specs=(row, state, state, state),
        check_vma=False,
    )
```

time: 413 us -> 331 us (0.80)
  Pallas kernels: 0 us -> 246 us
  waiting for transfers between devices: 230 us -> 13.2 us
  blocking collectives: 41.4 us -> 0 us
  local copies, waits for them, and re-layouts: 41.8 us -> 6.78 us
  other arithmetic: 42.9 us -> 21.9 us
  matrix products: 18.3 us -> 31.7 us
  between operations: 14.3 us -> 0.93 us
  starting transfers between devices: 23 us -> 10.4 us
    pallas_call x0 -> x1, Pallas kernels: none -> 246 us  [move(): pl.pallas_call(functools.partial(move_kernel, rows_dp, shards, kinds), ou...]
    all_to_all x5 -> x2, waiting for transfers between devices: 136 us -> 13.2 us  [swap(): return lax.all_to_all(blocks, 'dp', split_axis=0, concat_axis=0, tiled=True)]
    all_gather x1 -> x0, waiting for transfers between devices: 94.3 us -> none  [local(): columns = lax.all_gather(new_params[0], 'expert', axis=2, tiled=True)]
    all_to_all x1 -> x0, blocking collectives: 41.4 us -> none  [relocate(): lax.all_to_all(spread[source], 'dp', split_axis=0, concat_axis=0, tiled=T...]
    gather x5 -> x0, local copies, waits for them, and re-layouts: 18.8 us -> none  [the longest x2 10.8 us: relocate(): spread[source]]
    dot_general x2 -> x22, matrix products: 18.3 us -> 31.7 us  [the longest x8 11.2 us: into(): jnp.dot(arrived, weights[kind, z], preferred_element_type=jnp.float32)]
    all_to_all x5 -> x2, starting transfers between devices: 22.9 us -> 10.4 us  [swap(): return lax.all_to_all(blocks, 'dp', split_axis=0, concat_axis=0, tiled=True)]
    convert_element_type x3 -> x0, local copies, waits for them, and re-layouts: 12.2 us -> none  [the longest x1 5.53 us: local(): returned[slot_index].astype(jnp.float32).reshape(tok_rows, topk, features)]
  transfers between devices with their start and end apart: 6 -> 2, of which waited for: 5 -> 2; matrix products, arithmetic and copies ran while one was open for 15% -> 7% of each run, Pallas kernels for 0% -> 0%
where the time goes in v2:
time: 331 us; the launch traced here: 330 us
  Pallas kernels  246 us (74%)
  matrix products  31.7 us (10%)
  other arithmetic  21.9 us (7%)
  waiting for transfers between devices  13.2 us (4%)
  starting transfers between devices  10.4 us (3%)
  local copies, waits for them, and re-layouts  6.78 us (2%)
    pallas_call x1, Pallas kernels, move(): pl.pallas_call(functools.partial(move_kernel, rows_dp, shards, kinds), ou...  246 us
    all_to_all x2, waiting for transfers between devices, swap(): return lax.all_to_all(blocks, 'dp', split_axis=0, concat_axis=0, tiled=True)  13.2 us
    dot_general x8, matrix products, into(): jnp.dot(arrived, weights[kind, z], preferred_element_type=jnp.float32)  11.2 us
    dot_general x8, matrix products, local(): lax.dot_general(hidden[z], weights[2, z, start:start + half], (((1,), (1,...  11 us
    convert_element_type x1, other arithmetic, local(): own_second.astype(jnp.bfloat16)  10.8 us
    all_to_all x2, starting transfers between devices, swap(): return lax.all_to_all(blocks, 'dp', split_axis=0, concat_axis=0, tiled=True)  10.4 us
    broadcast_in_dim x1, other arithmetic, local(): new_second = moved_second.astype(jnp.float32)[None]  7.8 us
  transfers between devices with their start and end apart: 2, of which 2 were waited for; matrix products, arithmetic and copies ran while one was open for 7% of the time, Pallas kernels for 0%

profile of v2, /device:TPU:0, one launch (start us, length us, event | category | flops | bytes accessed | tf_op | source)
XLA Modules:
  0.0 330.4 jit_solution(9683267841636209273)
XLA Ops:
  0.6 0.0 copy-start
  0.6 0.8 select_reduce_fusion.2
  1.5 0.7 compare_select_fusion
  2.1 0.8 copy.14
  2.9 0.1 eq.71
  3.1 0.3 fusion.15
  3.4 0.1 select_reduce_fusion
  3.5 0.1 add.70
  3.6 0.2 slice_reduce_fusion.1
  3.8 0.7 select_reduce_fusion.1
  4.6 0.6 gather_fusion
  5.2 1.0 convolution_convert_fusion
  6.2 0.9 copy-done.3
  7.1 10.8 %fusion.4 = (bf16[3,2048,256]{2,1,0:T(8,128)(2,1)}, bf16[3,2048,256]{2,1,0:T(8,128)(2,1)}, bf16[3,2048,256]{2,1,0:T(8,128)(2,1)}) fusion(f32[1,3,2048,256]{3,2,1,0:T(8,128)} %param.17, bf16[1,3,2048,256]{3,2,1,0:T(8,128)(2,1)S(1)} %copy-done.3, f32[1,3,2048,256]{3,2,1,0:T(8,128)} %param.16, bf16[1,3,2048,256]{3,2,1,0:T(8,128)(2,1)} %param.14), kind=kLoop, calls=%fused_computation.9 | loop fusion | flops 26738688 | bytes 28311552 | tf_op jit(solution)/shard_map/convert_element_type | solution.py:331
  17.9 245.5 %shard_map.120 = (bf16[3,4,2048,256]{3,2,1,0:T(8,128)(2,1)}, bf16[3,2048,256]{2,1,0:T(8,128)(2,1)S(1)}, bf16[3,2048,256]{2,1,0:T(8,128)(2,1)}, bf16[8,80,2048]{2,1,0:T(8,128)(2,1)S(1)}) custom-call(s32[8]{0:T(128)S(1)} %gather_fusion, bf16[3,2048,256]{2,1,0:T(8,128)(2,1)} %get-tuple-element.15.params, bf16[3,2048,256]{2,1,0:T(8,128)(2,1)} %get-tuple-element.16.first, ...), custom_call_target="tpu_custom_call" | custom-call | tf_op jit(solution)/shard_map/pallas_call | solution.py:255
  263.4 2.2 convolution_multiply_fusion.5
  265.6 2.6 convolution_multiply_fusion.7
  268.3 2.1 convolution_multiply_fusion.3
  270.4 0.8 convolution_multiply_fusion.1
  271.2 0.9 fusion.13
  272.1 0.0 copy-start.4
  272.1 0.5 fusion.45
  272.6 0.9 fusion.14
  273.5 0.0 copy-start.5
  273.5 0.5 fusion.47
  274.1 0.9 fusion.12
  275.0 0.0 copy-start.7
  275.0 0.5 fusion.43
  275.5 0.2 copy-done.7
  275.7 0.9 fusion.11
  276.6 1.7 multiply_convert_fusion.1
  278.3 5.9 %all-to-all-start = ((bf16[8,80,1024]{2,1,0:T(8,128)(2,1)}), bf16[8,80,1024]{2,1,0:T(8,128)(2,1)}, u32[]{:S(2)}, u32[]{:S(2)}) async-start(bf16[8,80,1024]{2,1,0:T(8,128)(2,1)} %bitcast.115), calls=%async_computation | async-start | bytes 2621440 | tf_op jit(solution)/shard_map/all_to_all | solution.py:34
  284.2 0.0 copy-start.8
  284.2 1.7 fusion.38
  285.9 1.6 fusion.40
  287.5 1.6 fusion.36
  289.1 2.8 multiply_convert_fusion
  291.9 10.8 %all-to-all-done = bf16[8,80,1024]{2,1,0:T(8,128)(2,1)} async-done(((bf16[8,80,1024]{2,1,0:T(8,128)(2,1)}), bf16[8,80,1024]{2,1,0:T(8,128)(2,1)}, u32[]{:S(2)}, u32[]{:S(2)}) %all-to-all-start) | async-done | bytes 1310752 | tf_op jit(solution)/shard_map/all_to_all | solution.py:34
  302.7 4.5 %all-to-all-start.1 = ((bf16[8,80,1024]{2,1,0:T(8,128)(2,1)}), bf16[8,80,1024]{2,1,0:T(8,128)(2,1)}, u32[]{:S(2)}, u32[]{:S(2)}) async-start(bf16[8,80,1024]{2,1,0:T(8,128)(2,1)} %bitcast.114), calls=%async_computation.1 | async-start | bytes 2621440 | tf_op jit(solution)/shard_map/all_to_all | solution.py:34
  307.2 0.0 copy-start.9
  307.2 7.8 %bitcast_convert_fusion = (f32[1,3,2048,256]{3,2,1,0:T(8,128)}, f32[1,3,2048,256]{3,2,1,0:T(8,128)}) fusion(bf16[3,2048,256]{2,1,0:T(8,128)(2,1)} %get-tuple-element.11, bf16[3,2048,256]{2,1,0:T(8,128)(2,1)S(1)} %get-tuple-element.10), kind=kLoop, calls=%fused_computation.11 | loop fusion | flops 3145728 | bytes 18874368 | tf_op jit(solution)/shard_map/broadcast_in_dim | solution.py:339
  315.0 3.8 %dynamic-slice_bitcast_fusion = bf16[1,3,2048,256]{3,2,1,0:T(8,128)(2,1)} fusion(bf16[3,4,2048,256]{3,2,1,0:T(8,128)(2,1)} %get-tuple-element.9, s32[]{:T(128)S(6)} %select_n.36), kind=kLoop, calls=%fused_computation.13 | loop fusion | bytes 6291460 | tf_op jit(solution)/shard_map/broadcast_in_dim | solution.py:335
  318.8 2.0 fusion.64
  320.8 2.0 fusion.5
  322.8 2.4 all-to-all-done.1
  325.2 2.1 fusion.62
  327.3 2.0 fusion.6
  329.4 1.1 pad_maximum_fusion
  (15 shorter events, 0.0 us)
Async XLA Ops:
  0.6 4.6 %copy-start = (bf16[256,2048]{1,0:T(8,128)(2,1)S(1)}, bf16[256,2048]{1,0:T(8,128)(2,1)}, u32[]{:S(2)}) copy-start(bf16[256,2048]{1,0:T(8,128)(2,1)} %param.9) | copy-start | bytes 3145732
  5.2 1.9 copy-start.3
  263.4 7.0 %copy-start.2 = (bf16[3,4,2048,256]{3,2,1,0:T(8,128)(2,1)S(1)}, bf16[3,4,2048,256]{3,2,1,0:T(8,128)(2,1)}, u32[]{:S(2)}) copy-start(bf16[3,4,2048,256]{3,2,1,0:T(8,128)(2,1)} %get-tuple-element.9) | copy-start | bytes 37748740
  272.1 1.4 copy-start.4
  273.5 1.4 copy-start.5
  275.0 0.7 copy-start.7
  278.3 24.4 %all-to-all-start = ((bf16[8,80,1024]{2,1,0:T(8,128)(2,1)}), bf16[8,80,1024]{2,1,0:T(8,128)(2,1)}, u32[]{:S(2)}, u32[]{:S(2)}) async-start(bf16[8,80,1024]{2,1,0:T(8,128)(2,1)} %bitcast.115), calls=%async_computation | async-start | bytes 2621440 | tf_op jit(solution)/shard_map/all_to_all | solution.py:34
  284.2 1.8 copy-start.6
  284.2 3.3 %copy-start.8 = (bf16[640,256]{1,0:T(8,128)(2,1)S(1)}, bf16[640,256]{1,0:T(8,128)(2,1)}, u32[]{:S(2)}) copy-start(bf16[640,256]{1,0:T(8,128)(2,1)} %copy-done.7) | copy-start | bytes 983044
  302.7 22.5 %all-to-all-start.1 = ((bf16[8,80,1024]{2,1,0:T(8,128)(2,1)}), bf16[8,80,1024]{2,1,0:T(8,128)(2,1)}, u32[]{:S(2)}, u32[]{:S(2)}) async-start(bf16[8,80,1024]{2,1,0:T(8,128)(2,1)} %bitcast.114), calls=%async_computation.1 | async-start | bytes 2621440 | tf_op jit(solution)/shard_map/all_to_all | solution.py:34
  307.2 7.8 %copy-start.9 = (f32[256,2]{0,1:T(2,128)S(1)}, f32[256,2]{0,1:T(2,128)}, u32[]{:S(2)}) copy-start(f32[256,2]{0,1:T(2,128)} %param.11) | copy-start | bytes 6148
  325.2 5.2 %copy-start.1 = (bf16[256,2048]{1,0:T(8,128)(2,1)S(1)}, bf16[256,2048]{1,0:T(8,128)(2,1)}, u32[]{:S(2)}) copy-start(bf16[256,2048]{1,0:T(8,128)(2,1)} %param.9) | copy-start | bytes 3145732

commit v3 on v2

--- a/solution.py
+++ b/solution.py
@@ -61,6 +61,10 @@
     def rows(row):
         return pl.ds(pl.multiple_of(row * block, block), block)
 
+    def columns(shard):
+        width = params.shape[2]
+        return pl.ds(pl.multiple_of(shard * width, width), width)
+
     def remote(src, dst, send, recv, target):
         return pltpu.make_async_remote_copy(
             src_ref=src,
@@ -83,7 +87,7 @@
 
     def final(chunk, row):
         if chunk < kinds:
-            return weights.at[chunk, z, rows(row)]
+            return weights.at[chunk, rows(row), columns(z)]
         return (new_first, new_second)[chunk // kinds - 1].at[chunk % kinds, rows(row)]
 
     def one(chunk, peer, sender):
@@ -128,8 +132,8 @@
 
     def along(kind, shard, way):
         return remote(
-            weights.at[kind, shard],
-            weights.at[kind, shard],
+            weights.at[kind, :, columns(shard)],
+            weights.at[kind, :, columns(shard)],
             z_send.at[kind, shard, way],
             z_recv.at[kind, shard],
             {"expert": z + (1 if way == 0 else -1)},
@@ -255,7 +259,7 @@
     return pl.pallas_call(
         functools.partial(move_kernel, rows_dp, shards, kinds),
         out_shape=(
-            jax.ShapeDtypeStruct((kinds, shards, depth, width), jnp.bfloat16),
+            jax.ShapeDtypeStruct((kinds, depth, width * shards), jnp.bfloat16),
             state,
             state,
             jax.ShapeDtypeStruct(outgoing.shape, jnp.bfloat16),
@@ -296,7 +300,6 @@
     slots = experts * capacity
     kinds, depth, width = params.shape[1:]
     shards = lax.axis_size("expert")
-    half = features // 2
     source = inverse_of(old_place)[new_place]
 
     own_params, own_first, own_second = adam_update(
@@ -318,7 +321,7 @@
     mixing = sum(
         jnp.where(hits[k], gate_weights[:, k, None], 0.0) for k in range(topk)
     )
-    mixing_high = mixing.astype(jnp.bfloat16)
+    mixing_high = lax.reduce_precision(mixing, 8, 7).astype(jnp.bfloat16)
     mixing_low = (mixing - mixing_high.astype(jnp.float32)).astype(jnp.bfloat16)
 
     outgoing = lax.dot_general(
@@ -332,8 +335,8 @@
         outgoing.reshape(experts, capacity, features),
     )
     arrived = arrived.reshape(slots, features)
-    new_params = lax.dynamic_index_in_dim(
-        weights, lax.axis_index("expert"), axis=1, keepdims=False
+    new_params = lax.dynamic_slice_in_dim(
+        weights, lax.axis_index("expert") * width, width, axis=2
     )[None]
     new_first = moved_first.astype(jnp.float32)[None]
     new_second = moved_second.astype(jnp.float32)[None]
@@ -341,33 +344,29 @@
     in_scale = 1.0 / math.sqrt(features)
     out_scale = 1.0 / math.sqrt(width * shards)
 
-    def into(kind):
-        return [
-            jnp.dot(arrived, weights[kind, z], preferred_element_type=jnp.float32) * in_scale
-            for z in range(shards)
-        ]
-
-    gate_part, up_part = into(0), into(1)
-    hidden = [
-        (jax.nn.silu(gate) * up).astype(jnp.bfloat16) for gate, up in zip(gate_part, up_part)
-    ]
-    mixed = []
-    for start in (0, half):
-        summed = sum(
-            lax.dot_general(
-                hidden[z],
-                weights[2, z, start : start + half],
-                (((1,), (1,)), ((), ())),
-                preferred_element_type=jnp.float32,
-            )
-            for z in range(shards)
-        )
-        expert_out = (summed * out_scale).astype(jnp.bfloat16)
-        returned = swap(expert_out.reshape(experts, capacity, -1)).reshape(slots, -1)
-        total = jnp.dot(mixing_high, returned, preferred_element_type=jnp.float32)
-        total += jnp.dot(mixing_low, returned, preferred_element_type=jnp.float32)
-        mixed.append(total.astype(jnp.bfloat16))
-    return (jnp.concatenate(mixed, axis=1), new_params, new_first, new_second)
+    middle = features // 2
+    gate_part = jnp.dot(arrived, weights[0], preferred_element_type=jnp.float32) * in_scale
+    up_part = jnp.dot(arrived, weights[1], preferred_element_type=jnp.float32) * in_scale
+    hidden = (jax.nn.silu(gate_part) * up_part).astype(jnp.bfloat16)
+    expert_out = jnp.concatenate(
+        [
+            (
+                lax.dot_general(
+                    hidden,
+                    weights[2, start : start + middle],
+                    (((1,), (1,)), ((), ())),
+                    preferred_element_type=jnp.float32,
+                )
+                * out_scale
+            ).astype(jnp.bfloat16)
+            for start in (0, middle)
+        ],
+        axis=1,
+    )
+    returned = swap(expert_out.reshape(experts, capacity, features)).reshape(slots, features)
+    mixed = jnp.dot(mixing_high, returned, preferred_element_type=jnp.float32)
+    mixed += jnp.dot(mixing_low, returned, preferred_element_type=jnp.float32)
+    return (mixed.astype(jnp.bfloat16), new_params, new_first, new_second)
 
 
 def solution(mesh):

time: 331 us -> 323 us (0.976)
  matrix products: 31.7 us -> 19.5 us
  waiting for transfers between devices: 13.2 us -> 22.9 us
  starting transfers between devices: 10.4 us -> 5.99 us
    dot_general x20 -> x6, matrix products: 30.5 us -> 18.2 us  [the longest x1 4.86 us: local(): jnp.dot(arrived, weights[1], preferred_element_type=jnp.float32) * in_scale]
    all_to_all x2 -> x1, waiting for transfers between devices: 13.2 us -> 22.9 us  [swap(): return lax.all_to_all(blocks, 'dp', split_axis=0, concat_axis=0, tiled=True)]
    all_to_all x2 -> x1, starting transfers between devices: 10.4 us -> 5.99 us  [swap(): return lax.all_to_all(blocks, 'dp', split_axis=0, concat_axis=0, tiled=True)]
  transfers between devices with their start and end apart: 2 -> 1, of which waited for: 2 -> 1; matrix products, arithmetic and copies ran while one was open for 7% -> 3% of each run, Pallas kernels for 0% -> 0%
where the time goes in v3:
time: 323 us
  Pallas kernels  246 us (76%)
  waiting for transfers between devices  22.9 us (7%)
  other arithmetic  20.7 us (6%)
  matrix products  19.5 us (6%)
  local copies, waits for them, and re-layouts  7.69 us (2%)
  starting transfers between devices  5.99 us (2%)
    pallas_call x1, Pallas kernels, move(): pl.pallas_call(functools.partial(move_kernel, rows_dp, shards, kinds), ou...  246 us
    all_to_all x1, waiting for transfers between devices, swap(): return lax.all_to_all(blocks, 'dp', split_axis=0, concat_axis=0, tiled=True)  22.9 us
    convert_element_type x1, other arithmetic, local(): own_second.astype(jnp.bfloat16)  10.8 us
  transfers between devices with their start and end apart: 1, of which 1 were waited for; matrix products, arithmetic and copies ran while one was open for 3% of the time, Pallas kernels for 0%

profile of v3, /device:TPU:0, one launch (start us, length us, event | category | flops | bytes accessed | tf_op | source)
XLA Modules:
  0.0 323.0 jit_solution(10227768561323072559)
XLA Ops:
  0.6 0.0 copy-start
  0.6 0.8 select_reduce_fusion.2
  1.5 0.7 compare_select_fusion
  2.1 0.8 copy.14
  2.9 0.1 eq.71
  3.1 0.3 fusion.24
  3.4 0.1 select_reduce_fusion
  3.5 0.1 add.39
  3.6 0.2 slice_reduce_fusion.1
  3.8 0.7 select_reduce_fusion.1
  4.6 0.6 gather_fusion
  5.2 0.0 copy-start.2
  5.2 0.0 copy-done
  5.2 1.0 convolution_convert_fusion
  6.2 0.9 copy-done.2
  7.1 10.8 %fusion.10 = (bf16[3,2048,256]{2,1,0:T(8,128)(2,1)}, bf16[3,2048,256]{2,1,0:T(8,128)(2,1)}, bf16[3,2048,256]{2,1,0:T(8,128)(2,1)}) fusion(f32[1,3,2048,256]{3,2,1,0:T(8,128)} %param.17, bf16[1,3,2048,256]{3,2,1,0:T(8,128)(2,1)S(1)} %copy-done.2, f32[1,3,2048,256]{3,2,1,0:T(8,128)} %param.16, bf16[1,3,2048,256]{3,2,1,0:T(8,128)(2,1)} %param.14), kind=kLoop, calls=%fused_computation.15 | loop fusion | flops 26738688 | bytes 28311552 | tf_op jit(solution)/shard_map/convert_element_type | solution.py:334
  17.9 245.5 %shard_map.120 = (bf16[3,2048,1024]{2,1,0:T(8,128)(2,1)}, bf16[3,2048,256]{2,1,0:T(8,128)(2,1)S(1)}, bf16[3,2048,256]{2,1,0:T(8,128)(2,1)}, bf16[8,80,2048]{2,1,0:T(8,128)(2,1)S(1)}) custom-call(s32[8]{0:T(128)S(1)} %gather_fusion, bf16[3,2048,256]{2,1,0:T(8,128)(2,1)} %get-tuple-element.15.params, bf16[3,2048,256]{2,1,0:T(8,128)(2,1)} %get-tuple-element.16.first, ...), custom_call_target="tpu_custom_call" | custom-call | tf_op jit(solution)/shard_map/pallas_call | solution.py:259
  263.4 0.0 copy-start.4
  263.4 4.9 %fusion.3 = f32[640,1024]{1,0:T(8,128)S(1)} fusion(bf16[640,2048]{1,0:T(8,128)(2,1)S(1)} %bitcast.60, bf16[3,2048,1024]{2,1,0:T(8,128)(2,1)} %get-tuple-element.9), kind=kOutput, calls=%fused_computation.8 | convolution fusion | flops 2684354560 | bytes 9437184 | tf_op jit(solution)/shard_map/dot_general | solution.py:349
  268.3 1.0 copy-done.4
  269.2 3.4 %multiply_convert_fusion.2 = bf16[640,1024]{1,0:T(8,128)(2,1)S(1)} fusion(f32[640,1024]{1,0:T(8,128)S(1)} %fusion.3, bf16[640,2048]{1,0:T(8,128)(2,1)S(1)} %bitcast.61, bf16[3,2048,1024]{2,1,0:T(8,128)(2,1)S(1)} %copy-done.4), kind=kOutput, calls=%fused_computation.24 | convolution fusion | flops 2689597440 | bytes 10747904 | tf_op jit(solution)/shard_map/dot_general | solution.py:348
  272.6 1.6 multiply_convert_fusion.1
  274.2 1.6 multiply_convert_fusion
  275.8 1.7 pad_maximum_fusion
  277.5 0.0 copy-start.5
  277.5 6.0 %all-to-all-start = ((bf16[8,80,2048]{2,1,0:T(8,128)(2,1)}), bf16[8,80,2048]{2,1,0:T(8,128)(2,1)}, u32[]{:S(2)}, u32[]{:S(2)}) async-start(bf16[8,80,2048]{2,1,0:T(8,128)(2,1)} %bitcast.62), calls=%async_computation | async-start | bytes 5242880 | tf_op jit(solution)/shard_map/all_to_all | solution.py:34
  283.5 0.0 copy-done.5
  283.5 0.0 copy-start.3
  283.5 3.9 %dynamic-slice_bitcast_fusion = bf16[1,3,2048,256]{3,2,1,0:T(8,128)(2,1)} fusion(bf16[3,2048,1024]{2,1,0:T(8,128)(2,1)} %get-tuple-element.9, s32[]{:T(128)S(6)} %select_n.35), kind=kLoop, calls=%fused_computation.19 | loop fusion | bytes 6291460 | tf_op jit(solution)/shard_map/broadcast_in_dim | solution.py:338
  287.4 0.0 copy-done.3
  287.4 5.9 %bitcast_convert_fusion = (f32[1,3,2048,256]{3,2,1,0:T(8,128)}, f32[1,3,2048,256]{3,2,1,0:T(8,128)}) fusion(bf16[3,2048,256]{2,1,0:T(8,128)(2,1)S(1)} %copy-done.3, bf16[3,2048,256]{2,1,0:T(8,128)(2,1)S(1)} %get-tuple-element.10), kind=kLoop, calls=%fused_computation.17 | loop fusion | flops 3145728 | bytes 18874368 | tf_op jit(solution)/shard_map/broadcast_in_dim | solution.py:342
  293.3 22.9 %all-to-all-done = bf16[8,80,2048]{2,1,0:T(8,128)(2,1)} async-done(((bf16[8,80,2048]{2,1,0:T(8,128)(2,1)}), bf16[8,80,2048]{2,1,0:T(8,128)(2,1)}, u32[]{:S(2)}, u32[]{:S(2)}) %all-to-all-start) | async-done | bytes 2621472 | tf_op jit(solution)/shard_map/all_to_all | solution.py:34
  316.2 0.0 copy-start.1
  316.2 2.9 fusion.37
  319.1 3.9 %fusion.11 = bf16[256,2048]{1,0:T(8,128)(2,1)} fusion(f32[256,2048]{1,0:T(8,128)S(1)} %fusion.37, bf16[640,2048]{1,0:T(8,128)(2,1)} %bitcast.14, f32[256]{0:T(256)S(1)} %bitcast.66, s32[256]{0:T(256)S(1)} %get-tuple-element.13, f32[256]{0:T(256)S(1)} %bitcast.64, s32[256]{0:T(256)S(1)} %get-tuple-element.12), kind=kOutput, calls=%fused_computation.25 | convolution fusion | flops 673775616 | bytes 5771264 | tf_op jit(solution)/shard_map/dot_general | solution.py:368
  323.0 0.0 copy-done.1
  (3 shorter events, 0.0 us)
Async XLA Ops:
  0.6 4.6 %copy-start = (bf16[256,2048]{1,0:T(8,128)(2,1)S(1)}, bf16[256,2048]{1,0:T(8,128)(2,1)}, u32[]{:S(2)}) copy-start(bf16[256,2048]{1,0:T(8,128)(2,1)} %param.9) | copy-start | bytes 3145732
  5.2 1.9 copy-start.2
  263.4 5.8 %copy-start.4 = (bf16[3,2048,1024]{2,1,0:T(8,128)(2,1)S(1)}, bf16[3,2048,1024]{2,1,0:T(8,128)(2,1)}, u32[]{:S(2)}) copy-start(bf16[3,2048,1024]{2,1,0:T(8,128)(2,1)} %get-tuple-element.9) | copy-start | bytes 37748740
  277.5 6.0 %copy-start.5 = (f32[256,2]{0,1:T(2,128)S(1)}, f32[256,2]{0,1:T(2,128)}, u32[]{:S(2)}) copy-start(f32[256,2]{0,1:T(2,128)} %param.11) | copy-start | bytes 6148
  277.5 38.7 %all-to-all-start = ((bf16[8,80,2048]{2,1,0:T(8,128)(2,1)}), bf16[8,80,2048]{2,1,0:T(8,128)(2,1)}, u32[]{:S(2)}, u32[]{:S(2)}) async-start(bf16[8,80,2048]{2,1,0:T(8,128)(2,1)} %bitcast.62), calls=%async_computation | async-start | bytes 5242880 | tf_op jit(solution)/shard_map/all_to_all | solution.py:34
  283.5 3.9 %copy-start.3 = (bf16[3,2048,256]{2,1,0:T(8,128)(2,1)S(1)}, bf16[3,2048,256]{2,1,0:T(8,128)(2,1)}, u32[]{:S(2)}) copy-start(bf16[3,2048,256]{2,1,0:T(8,128)(2,1)} %get-tuple-element.11) | copy-start | bytes 9437188
  316.2 6.8 %copy-start.1 = (bf16[256,2048]{1,0:T(8,128)(2,1)S(1)}, bf16[256,2048]{1,0:T(8,128)(2,1)}, u32[]{:S(2)}) copy-start(bf16[256,2048]{1,0:T(8,128)(2,1)} %param.9) | copy-start | bytes 3145732
